TPU v7x, 32 devices: a whole 2x2x4 slice. The times are simulated.
32 devices in a mesh: grp: 2 (over y), pencil: 4 (over z), depth: 2 (over x), mem: 2 (over core).
Axes of the slice: x: 2, y: 2, z: 4, core: 2. Of those that a mesh axis runs over, the one named last changes fastest.
Arguments:
- density: float32 [4, 2, 2048, 2048], P(('grp', 'mem'), 'depth', 'pencil'), parts along dimension 0, may hold values from -6 to 6
- background: float32 [8, 2], P(None, 'depth'), may hold values from -2 to 2
- member_ids: int32 [4], P(('grp', 'mem')), parts along dimension 0, may hold values from 0 to 7
- layer_kernel: int32 [2], P('depth'), may hold values from 0 to 3, as said below
- kernel_spectra: bfloat16 [4, 2, 2048, 2048], P('depth', None, None, 'pencil'), may hold values from -4 to 4
Outputs:
- gravity: float32 [4, 2048, 2048], P(('grp', 'mem'), ('pencil', 'depth')), parts along dimension 0
There are 2 independent parts, one for each index of `grp`. A program takes and returns all parts, laid end to end along the dimension named above; an argument that names none is the same for every part. Nothing has to cross between parts.
Inputs may be any that keep to these rules, and one draw needn't show every extreme that they name: Layer l takes one of the 2 kernels of its depth band: layer_kernel[l] // 2 equals l.
All inputs are finite; a program needn't handle non-finite values.
Results may differ from a plain program's by a relative error of at most 0.0003.
Values sent between devices are 32-bit elements; how exact they have to be, the bound alone decides.
A program may use at most 128 MiB of HBM per device.

v0:
```python
import math
import jax
import jax.numpy as jnp
from jax import lax
from jax.sharding import PartitionSpec as P

base_radix = 16
highest = lax.Precision.HIGHEST


def twiddle_table(row_count, col_count, modulus):
    left_index = lax.broadcasted_iota(jnp.int32, (row_count, col_count), 0)
    right_index = lax.broadcasted_iota(jnp.int32, (row_count, col_count), 1)
    angles = (left_index * right_index % modulus).astype(jnp.float32) * (2.0 * math.pi / modulus)
    return (jnp.cos(angles), jnp.sin(angles))


def forward_rows(values):
    leading = values.shape[:-1]
    length = values.shape[-1]
    inner_len = length // base_radix
    blocks = values.reshape(leading + (base_radix, inner_len))
    cos_small, sin_small = twiddle_table(base_radix, base_radix, base_radix)
    first_real = jnp.einsum("kn,...nm->...km", cos_small, blocks, precision=highest)
    first_imag = -jnp.einsum("kn,...nm->...km", sin_small, blocks, precision=highest)
    cos_turn, sin_turn = twiddle_table(base_radix, inner_len, length)
    turned_real = first_real * cos_turn + first_imag * sin_turn
    turned_imag = first_imag * cos_turn - first_real * sin_turn
    cos_large, sin_large = twiddle_table(inner_len, inner_len, inner_len)
    final_real = jnp.einsum(
        "...kn,nm->...km", turned_real, cos_large, precision=highest
    ) + jnp.einsum("...kn,nm->...km", turned_imag, sin_large, precision=highest)
    final_imag = jnp.einsum(
        "...kn,nm->...km", turned_imag, cos_large, precision=highest
    ) - jnp.einsum("...kn,nm->...km", turned_real, sin_large, precision=highest)
    return (final_real.reshape(leading + (length,)), final_imag.reshape(leading + (length,)))


def forward_columns(real_part, imag_part):
    leading = real_part.shape[:-2]
    length = real_part.shape[-2]
    col_width = real_part.shape[-1]
    inner_len = length // base_radix
    block_shape = leading + (base_radix, inner_len, col_width)
    split_real = real_part.reshape(block_shape)
    split_imag = imag_part.reshape(block_shape)
    cos_small, sin_small = twiddle_table(base_radix, base_radix, base_radix)
    first_real = jnp.einsum(
        "kn,...nmq->...kmq", cos_small, split_real, precision=highest
    ) + jnp.einsum("kn,...nmq->...kmq", sin_small, split_imag, precision=highest)
    first_imag = jnp.einsum(
        "kn,...nmq->...kmq", cos_small, split_imag, precision=highest
    ) - jnp.einsum("kn,...nmq->...kmq", sin_small, split_real, precision=highest)
    cos_turn, sin_turn = twiddle_table(base_radix, inner_len, length)
    cos_turn = cos_turn[:, :, None]
    sin_turn = sin_turn[:, :, None]
    turned_real = first_real * cos_turn + first_imag * sin_turn
    turned_imag = first_imag * cos_turn - first_real * sin_turn
    cos_large, sin_large = twiddle_table(inner_len, inner_len, inner_len)
    final_real = jnp.einsum(
        "...kmq,mj->...kjq", turned_real, cos_large, precision=highest
    ) + jnp.einsum("...kmq,mj->...kjq", turned_imag, sin_large, precision=highest)
    final_imag = jnp.einsum(
        "...kmq,mj->...kjq", turned_imag, cos_large, precision=highest
    ) - jnp.einsum("...kmq,mj->...kjq", turned_real, sin_large, precision=highest)
    out_shape = leading + (length, col_width)
    return (final_real.reshape(out_shape), final_imag.reshape(out_shape))


def inverse_columns(real_part, imag_part):
    length = real_part.shape[0]
    col_width = real_part.shape[1]
    inner_len = length // base_radix
    split_real = real_part.reshape(base_radix, inner_len, col_width)
    split_imag = imag_part.reshape(base_radix, inner_len, col_width)
    cos_large, sin_large = twiddle_table(inner_len, inner_len, inner_len)
    first_real = jnp.einsum("kmq,mj->kjq", split_real, cos_large, precision=highest) - jnp.einsum(
        "kmq,mj->kjq", split_imag, sin_large, precision=highest
    )
    first_imag = jnp.einsum("kmq,mj->kjq", split_imag, cos_large, precision=highest) + jnp.einsum(
        "kmq,mj->kjq", split_real, sin_large, precision=highest
    )
    cos_turn, sin_turn = twiddle_table(base_radix, inner_len, length)
    cos_turn = cos_turn[:, :, None]
    sin_turn = sin_turn[:, :, None]
    turned_real = first_real * cos_turn - first_imag * sin_turn
    turned_imag = first_imag * cos_turn + first_real * sin_turn
    cos_small, sin_small = twiddle_table(base_radix, base_radix, base_radix)
    final_real = jnp.einsum("nk,kjq->njq", cos_small, turned_real, precision=highest) - jnp.einsum(
        "nk,kjq->njq", sin_small, turned_imag, precision=highest
    )
    final_imag = jnp.einsum("nk,kjq->njq", cos_small, turned_imag, precision=highest) + jnp.einsum(
        "nk,kjq->njq", sin_small, turned_real, precision=highest
    )
    return (final_real.reshape(length, col_width), final_imag.reshape(length, col_width))


def inverse_rows(real_part, imag_part):
    row_count = real_part.shape[0]
    length = real_part.shape[1]
    inner_len = length // base_radix
    split_real = real_part.reshape(row_count, base_radix, inner_len)
    split_imag = imag_part.reshape(row_count, base_radix, inner_len)
    cos_large, sin_large = twiddle_table(inner_len, inner_len, inner_len)
    first_real = jnp.einsum("rkm,mj->rkj", split_real, cos_large, precision=highest) - jnp.einsum(
        "rkm,mj->rkj", split_imag, sin_large, precision=highest
    )
    first_imag = jnp.einsum("rkm,mj->rkj", split_imag, cos_large, precision=highest) + jnp.einsum(
        "rkm,mj->rkj", split_real, sin_large, precision=highest
    )
    cos_turn, sin_turn = twiddle_table(base_radix, inner_len, length)
    turned_real = first_real * cos_turn - first_imag * sin_turn
    turned_imag = first_imag * cos_turn + first_real * sin_turn
    cos_small, sin_small = twiddle_table(base_radix, base_radix, base_radix)
    final_real = jnp.einsum("nk,rkj->rnj", cos_small, turned_real, precision=highest) - jnp.einsum(
        "nk,rkj->rnj", sin_small, turned_imag, precision=highest
    )
    return final_real.reshape(row_count, length)


def body(density, background, member_ids, layer_kernel, kernel_spectra):
    profiles = background.shape[0]
    chosen = (lax.broadcasted_iota(jnp.int32, (profiles,), 0) == member_ids[0]).astype(jnp.float32)
    offsets = jnp.dot(chosen, background, precision=highest)
    contrast = density[0] - offsets[:, None, None]
    row_real, row_imag = forward_rows(contrast)
    paired = jnp.stack([row_real, row_imag], axis=1)
    layer_block = lax.all_to_all(paired, "pencil", split_axis=3, concat_axis=2, tiled=True)
    out_real, out_imag = forward_columns(layer_block[:, 0], layer_block[:, 1])
    spectra = jnp.stack([out_real, out_imag], axis=1)
    kern_count = kernel_spectra.shape[0]
    layer_count = layer_kernel.shape[0]
    band_start = lax.axis_index("depth") * kern_count
    local_index = layer_kernel - band_start
    weights = (
        local_index[:, None] == lax.broadcasted_iota(jnp.int32, (layer_count, kern_count), 1)
    ).astype(jnp.float32)
    binned = jnp.einsum("lk,lcxq->kcxq", weights, spectra, precision=highest)
    kernels = kernel_spectra.astype(jnp.float32)
    part_real = jnp.sum(binned[:, 0] * kernels[:, 0] - binned[:, 1] * kernels[:, 1], axis=0)
    part_imag = jnp.sum(binned[:, 0] * kernels[:, 1] + binned[:, 1] * kernels[:, 0], axis=0)
    partial_value = jnp.stack([part_real, part_imag], axis=0)
    depth_count = lax.axis_size("depth")
    pencil_count = lax.axis_size("pencil")
    length_x = partial_value.shape[1]
    col_width = partial_value.shape[2]
    rows_out = length_x // (pencil_count * depth_count)
    summed = lax.psum(partial_value, "depth")
    field_real, field_imag = inverse_columns(summed[0], summed[1])
    stacked = jnp.stack([field_real, field_imag], axis=1)
    own_rows = lax.dynamic_index_in_dim(
        stacked.reshape(pencil_count, depth_count, rows_out, 2, col_width),
        lax.axis_index("depth"),
        1,
        keepdims=False,
    )
    gathered = lax.all_to_all(own_rows, "pencil", split_axis=0, concat_axis=3, tiled=True)
    grid_rows = gathered[0]
    result = inverse_rows(grid_rows[:, 0], grid_rows[:, 1]) * (
        1.0 / (length_x * grid_rows.shape[-1])
    )
    return result[None]


def solution(mesh):
    placed = (
        P(("grp", "mem"), "depth", "pencil", None),
        P(None, "depth"),
        P(("grp", "mem")),
        P("depth"),
        P("depth", None, None, "pencil"),
    )
    return jax.shard_map(
        body,
        mesh=mesh,
        in_specs=placed,
        out_specs=P(("grp", "mem"), ("pencil", "depth"), None),
        check_vma=False,
    )
```

profile of v0, /device:TPU:0, one launch (start us, length us, event | category | flops | bytes accessed | tf_op | source)
XLA Modules:
  0.0 762.8 jit_solution(689112349098130173)
XLA Ops:
  6.5 0.1 fusion.143
  7.2 1.3 fusion.160
  8.6 3.1 subtract_bitcast_fusion
  11.7 0.9 copy.187
  12.6 3.9 fusion.128
  16.6 4.8 fusion.8
  21.4 5.9 fusion.35
  27.3 5.7 fusion.37
  32.9 6.1 fusion.43
  39.0 5.8 fusion.46
  44.8 8.0 %copy.122 = f32[1,1,512,2048]{2,1,0,3:T(1,128)S(1)} copy(f32[1,1,512,2048]{2,3,1,0:T(8,128)S(1)} %bitcast.222) | data formatting | bytes 8388608 | tf_op jit(solution)/shard_map/stack;reshape | solution.py:127
  52.8 8.0 %copy.121 = f32[1,1,512,2048]{2,1,0,3:T(1,128)S(1)} copy(f32[1,1,512,2048]{2,3,1,0:T(8,128)S(1)} %bitcast.221) | data formatting | bytes 8388608 | tf_op jit(solution)/shard_map/stack;reshape | solution.py:127
  60.8 8.8 %pad_maximum_fusion = f32[1,2,512,2048]{2,1,0,3:T(2,128)} fusion(f32[1,1,512,2048]{2,1,0,3:T(1,128)S(1)} %copy.122, f32[1,1,512,2048]{2,1,0,3:T(1,128)S(1)} %copy.121), kind=kLoop, calls=%fused_computation | loop fusion | flops 2097152 | bytes 16777216 | tf_op jit(solution)/shard_map/stack | solution.py:127
  69.6 6.3 all-to-all-start
  75.9 0.0 all-reduce.2.cloned.1.call-start
  75.9 0.1 copy.130
  76.0 0.1 copy.127
  76.8 11.5 %convert_element_type.136 = f32[2,2,2048,512]{3,2,1,0:T(8,128)} convert(bf16[2,2,2048,512]{3,2,1,0:T(8,128)(2,1)} %param.9) | non-fusion elementwise | flops 4194304 | bytes 25165824 | tf_op jit(solution)/shard_map/convert_element_type | solution.py:139
  88.3 171.7 %all-to-all-done = f32[1,2,512,2048]{2,1,0,3:T(2,128)} async-done(((f32[1,2,512,2048]{2,1,0,3:T(2,128)}), f32[1,2,512,2048]{2,1,0,3:T(2,128)}, u32[]{:S(2)}, u32[]{:S(2)}) %all-to-all-start) | async-done | bytes 8388640 | tf_op jit(solution)/shard_map/all_to_all | solution.py:128
  260.0 8.2 %copy.123 = f32[1,2,512,2048]{2,3,1,0:T(8,128)} copy(f32[1,2,512,2048]{2,1,0,3:T(2,128)} %all-to-all-done) | data formatting | bytes 16777216 | tf_op jit(solution)/shard_map/all_to_all | solution.py:128
  268.2 10.0 %copy.124 = f32[1,2,4,512,512]{4,3,2,1,0:T(8,128)} copy(f32[1,2,4,512,512]{3,4,2,1,0:T(8,128)} %bitcast.216) | data formatting | bytes 16777216 | tf_op jit(solution)/shard_map/all_to_all | solution.py:128
  278.2 4.4 fusion.274
  282.7 6.8 fusion.27
  289.5 6.8 fusion.29
  296.3 7.2 fusion.49
  303.5 8.9 %fusion.4 = (f32[16,128,512]{2,0,1:T(8,128)S(1)}, f32[16,128,512]{2,0,1:T(8,128)S(1)}) fusion(f32[128,512,16]{1,2,0:T(8,128)S(1)} %fusion.49, f32[16,128]{0,1:T(8,128)S(1)} %copy.130, f32[16,128]{0,1:T(8,128)S(1)} %copy.127, f32[128,512,16]{1,2,0:T(8,128)S(1)} %fusion.27, f32[16,128,512]{2,1,0:T(8,128)S(1)} %bitcast.206), kind=kOutput, calls=%fused_computation.18 | convolution fusion | flops 208670208 | bytes 20987904 | tf_op jit(solution)/shard_map/kn,...nmq->...kmq/dot_general | solution.py:53
  312.4 6.1 fusion.19
  318.5 6.5 fusion.21
  325.1 6.4 fusion.55
  331.5 6.7 fusion.58
  338.2 4.2 maximum_bitcast_fusion
  342.4 11.4 %broadcast_multiply_fusion = f32[2,2,2048,512]{3,2,1,0:T(8,128)} fusion(f32[2,2048,512]{2,1,0:T(8,128)} %maximum_bitcast_fusion, f32[2]{0:T(128)S(1)} %fusion.159), kind=kLoop, calls=%fused_computation.7 | loop fusion | flops 4194304 | bytes 25165832 | tf_op jit(solution)/shard_map/lk,lcxq->kcxq/dot_general | solution.py:138
  353.8 17.3 %subtract_reduce_fusion = (f32[2048,512]{1,0:T(8,128)}, f32[2048,512]{1,0:T(8,128)}) fusion(f32[2,2,2048,512]{3,2,1,0:T(8,128)} %convert_element_type.136, f32[2,2,2048,512]{3,2,1,0:T(8,128)} %broadcast_multiply_fusion), kind=kLoop, calls=%fused_computation.6 | loop fusion | flops 14680064 | bytes 41943040 | tf_op jit(solution)/shard_map/reduce_sum | solution.py:140
  371.1 7.7 %pad_maximum_fusion.1 = f32[2,2048,512]{2,1,0:T(8,128)} fusion(f32[1,2048,512]{2,1,0:T(8,128)} %bitcast.225, f32[1,2048,512]{2,1,0:T(8,128)} %bitcast.224), kind=kLoop, calls=%fused_computation.2 | loop fusion | flops 2097152 | bytes 16777216 | tf_op jit(solution)/shard_map/stack | solution.py:142
  378.8 0.0 all-reduce.2.cloned.1.call-update
  378.8 197.3 %all-reduce.2.cloned.1.call-done = f32[2,2048,512]{2,1,0:T(8,128)} async-done(((f32[2,2048,512]{2,1,0:T(8,128)}), f32[2,2048,512]{2,1,0:T(8,128)}) %all-reduce.2.cloned.1.call-update) | async-done | bytes 8388624 | tf_op jit(solution)/shard_map/psum | solution.py:148
  576.1 4.4 fusion.273
  580.6 4.3 fusion.88
  584.9 4.1 fusion.94
  589.0 4.6 convolution_subtract_fusion
  593.5 5.3 fusion.1
  598.9 6.0 fusion.11
  604.9 5.6 fusion.13
  610.5 6.1 fusion.61
  616.6 5.7 fusion.64
  622.3 2.4 copy.148
  624.7 2.4 copy.145
  627.1 0.6 copy_bitcast_fusion
  627.8 97.6 %all_to_all.33 = f32[4,256,2,512]{3,1,2,0:T(8,128)} all-to-all(f32[4,256,2,512]{3,1,2,0:T(8,128)S(1)} %copy_bitcast_fusion), channel_id=1, replica_groups=mesh['grp'=2,'pencil'=4,'depth'=2,'mem'=2] {'pencil'}, dimensions={0} | all-to-all | bytes 8388608 | tf_op jit(solution)/shard_map/all_to_all | solution.py:157
  725.4 5.2 copy.150
  730.7 2.5 fusion.275
  733.2 3.7 fusion.86
  736.8 3.6 fusion.84
  740.4 3.6 convolution_subtract_fusion.1
  744.1 4.0 multiply_subtract_fusion
  748.0 3.1 fusion.67
  751.1 3.2 multiply_bitcast_fusion
  754.3 1.5 mul.460
  (1 shorter events, 0.0 us)
Async XLA Ops:
  69.6 190.4 %all-to-all-start = ((f32[1,2,512,2048]{2,1,0,3:T(2,128)}), f32[1,2,512,2048]{2,1,0,3:T(2,128)}, u32[]{:S(2)}, u32[]{:S(2)}) async-start(f32[1,2,512,2048]{2,1,0,3:T(2,128)} %pad_maximum_fusion), calls=%async_computation | async-start | bytes 16777216 | tf_op jit(solution)/shard_map/all_to_all | solution.py:128
  75.9 500.2 %all-reduce.2.cloned.1.call-start = ((), (), s32[]{:S(2)}) async-start(), calls=%async_computation.2 | async-start | bytes 16777216 | tf_op jit(solution)/shard_map/psum | solution.py:148
Sparse Core Ops, SparseCore 0:
  378.9 197.1 all-reduce.1
where the time goes:
time: 772 us; the launch traced here: 763 us
  waiting for transfers between devices  369 us (48%)
  matrix products  150 us (19%)
  blocking collectives  97.6 us (13%)
  other arithmetic  66 us (9%)
  local copies, waits for them, and re-layouts  58.4 us (8%)
  between operations  15.2 us (2%)
    psum x1, waiting for transfers between devices, body(): summed = lax.psum(partial_value, 'depth')  197 us
    all_to_all x1, waiting for transfers between devices, body(): lax.all_to_all(paired, 'pencil', split_axis=3, concat_axis=2, tiled=True)  172 us
    all_to_all x1, blocking collectives, body(): lax.all_to_all(own_rows, 'pencil', split_axis=0, concat_axis=3, tiled=True)  97.6 us
    all_to_all x2, local copies, waits for them, and re-layouts, body(): lax.all_to_all(paired, 'pencil', split_axis=3, concat_axis=2, tiled=True)  18.2 us
    reduce_sum x1, other arithmetic, body(): jnp.sum(binned[:, 0] * kernels[:, 0] - binned[:, 1] * kernels[:, 1], axis=0)  17.3 us
    another operation x2, local copies, waits for them, and re-layouts, body(): paired = jnp.stack([row_real, row_imag], axis=1)  16 us
  transfers between devices with their start and end apart: 2, of which 2 were waited for; matrix products, arithmetic and copies ran while one was open for 2% of the time, Pallas kernels for 0%

commit v1 on v0

--- a/solution.py
+++ b/solution.py
@@ -6,6 +6,17 @@
 
 base_radix = 16
 highest = lax.Precision.HIGHEST
+
+
+def in_blocks(value, dim, devices):
+    before, after = (value.shape[:dim], value.shape[dim + 1 :])
+    return jnp.moveaxis(value.reshape(*before, devices, -1, *after), dim, 0)
+
+
+def laid_out(pieces, dim):
+    lengths = list(pieces.shape[1:])
+    lengths[dim] *= pieces.shape[0]
+    return jnp.moveaxis(pieces, 0, dim).reshape(lengths)
 
 
 def twiddle_table(row_count, col_count, modulus):
@@ -125,7 +136,14 @@
     contrast = density[0] - offsets[:, None, None]
     row_real, row_imag = forward_rows(contrast)
     paired = jnp.stack([row_real, row_imag], axis=1)
-    layer_block = lax.all_to_all(paired, "pencil", split_axis=3, concat_axis=2, tiled=True)
+    size, index = (lax.axis_size("pencil"), lax.axis_index("pencil"))
+    blocks_2 = in_blocks(paired, 3, size)
+    outs = [blocks_2[index]]
+    for step in range(1, size):
+        sent = blocks_2[index ^ step]
+        outs.append(lax.ppermute(sent, "pencil", [(i, i ^ step) for i in range(size)]))
+    blocks_2 = jnp.stack(outs)[index ^ jnp.arange(size)]
+    layer_block = laid_out(blocks_2, 2)
     out_real, out_imag = forward_columns(layer_block[:, 0], layer_block[:, 1])
     spectra = jnp.stack([out_real, out_imag], axis=1)
     kern_count = kernel_spectra.shape[0]

time: 772 us -> 752 us (0.974)
  local copies, waits for them, and re-layouts: 58.4 us -> 43.3 us
  waiting for transfers between devices: 369 us -> 358 us
    all_to_all x1 -> x0, waiting for transfers between devices: 172 us -> none  [body(): lax.all_to_all(paired, 'pencil', split_axis=3, concat_axis=2, tiled=True)]
    ppermute x0 -> x3, waiting for transfers between devices: none -> 159 us  [body(): lax.ppermute(sent, 'pencil', [(i, i ^ step) for i in range(size)])]
    all_to_all x2 -> x0, local copies, waits for them, and re-layouts: 18.2 us -> none  [body(): lax.all_to_all(paired, 'pencil', split_axis=3, concat_axis=2, tiled=True)]
    another operation x2 -> x4, local copies, waits for them, and re-layouts: 16 us -> 10.5 us  [body(): paired = jnp.stack([row_real, row_imag], axis=1)]
  transfers between devices with their start and end apart: 2 -> 4, of which waited for: 2 -> 3; matrix products, arithmetic and copies ran while one was open for 2% -> 3% of each run, Pallas kernels for 0% -> 0%
where the time goes in v1:
time: 752 us; the launch traced here: 743 us
  waiting for transfers between devices  358 us (48%)
  matrix products  154 us (20%)
  blocking collectives  97.6 us (13%)
  other arithmetic  69.4 us (9%)
  local copies, waits for them, and re-layouts  43.3 us (6%)
  between operations  15.4 us (2%)
    psum x1, waiting for transfers between devices, body(): summed = lax.psum(partial_value, 'depth')  198 us
    ppermute x3, waiting for transfers between devices, body(): lax.ppermute(sent, 'pencil', [(i, i ^ step) for i in range(size)])  159 us
    all_to_all x1, blocking collectives, body(): lax.all_to_all(own_rows, 'pencil', split_axis=0, concat_axis=3, tiled=True)  97.6 us
    reduce_sum x1, other arithmetic, body(): jnp.sum(binned[:, 0] * kernels[:, 0] - binned[:, 1] * kernels[:, 1], axis=0)  17.1 us
  transfers between devices with their start and end apart: 4, of which 3 were waited for; matrix products, arithmetic and copies ran while one was open for 3% of the time, Pallas kernels for 0%

profile of v1, /device:TPU:0, one launch (start us, length us, event | category | flops | bytes accessed | tf_op | source)
XLA Modules:
  0.0 742.7 jit_solution(319729114763775752)
XLA Ops:
  6.5 0.1 fusion.147
  7.2 1.3 fusion.192
  8.5 3.0 subtract_bitcast_fusion
  11.6 0.9 copy.147
  12.5 3.9 fusion.132
  16.4 4.8 fusion.8
  21.2 5.9 fusion.35
  27.1 5.5 fusion.37
  32.6 7.8 %fusion.43 = f32[512,16,128]{0,2,1:T(8,128)} fusion(f32[512,16,128]{0,2,1:T(8,128)S(1)} %fusion.37, f32[512,16,128]{2,1,0:T(8,128)S(1)} %get-tuple-element.11), kind=kOutput, calls=%fused_computation.74 | convolution fusion | flops 1611890688 | bytes 12582912 | tf_op jit(solution)/shard_map/...kn,nm->...km/dot_general | solution.py:41
  40.4 7.5 %fusion.46 = f32[512,16,128]{0,2,1:T(8,128)} fusion(f32[512,16,128]{0,2,1:T(8,128)S(1)} %fusion.35, f32[512,16,128]{2,1,0:T(8,128)S(1)} %get-tuple-element.11), kind=kOutput, calls=%fused_computation.75 | convolution fusion | flops 1611890688 | bytes 12582912 | tf_op jit(solution)/shard_map/...kn,nm->...km/dot_general | solution.py:46
  48.0 6.7 fusion.68
  54.7 2.9 copy.83
  57.6 5.1 collective-permute-start.2
  62.7 2.9 copy.82
  65.5 0.0 collective-permute-start.1
  65.6 2.9 copy.81
  68.5 0.6 collective-permute-start
  69.0 0.1 copy.90
  69.1 0.1 copy.87
  69.9 1.8 copy.80
  71.7 11.6 %convert_element_type.136 = f32[2,2,2048,512]{3,2,1,0:T(8,128)} convert(bf16[2,2,2048,512]{3,2,1,0:T(8,128)(2,1)} %param.9) | non-fusion elementwise | flops 4194304 | bytes 25165824 | tf_op jit(solution)/shard_map/convert_element_type | solution.py:157
  83.4 26.2 %collective-permute-done.2 = f32[1,2,512,512]{3,2,1,0:T(8,128)} collective-permute-done((f32[1,2,512,512]{3,2,1,0:T(8,128)}, f32[1,2,512,512]{3,2,1,0:T(8,128)}, u32[]{:S(2)}, u32[]{:S(2)}) %collective-permute-start.2) | collective-permute-done | bytes 2097184 | tf_op jit(solution)/shard_map/ppermute | solution.py:144
  109.6 133.0 %collective-permute-done.1 = f32[1,2,512,512]{3,2,1,0:T(8,128)} collective-permute-done((f32[1,2,512,512]{3,2,1,0:T(8,128)}, f32[1,2,512,512]{3,2,1,0:T(8,128)}, u32[]{:S(2)}, u32[]{:S(2)}) %collective-permute-start.1) | collective-permute-done | bytes 2097184 | tf_op jit(solution)/shard_map/ppermute | solution.py:144
  242.6 0.0 collective-permute-done
  242.6 5.7 maximum_bitcast_fusion
  248.3 7.7 %gather_fusion = f32[4,2,512,512]{3,2,1,0:T(8,128)} fusion(f32[4,2,512,512]{3,2,1,0:T(8,128)} %maximum_bitcast_fusion, s32[1024]{0:T(1024)S(1)} %pad_clamp_fusion), kind=kCustom, calls=%fused_computation | custom fusion | bytes 16777232 | tf_op jit(solution)/shard_map/gather | solution.py:145
  256.0 4.4 copy.84
  260.4 1.0 fusion.279
  261.4 6.8 fusion.27
  268.2 6.8 fusion.29
  275.0 7.2 fusion.49
  282.2 8.9 %fusion.4 = (f32[16,128,512]{2,0,1:T(8,128)S(1)}, f32[16,128,512]{2,0,1:T(8,128)S(1)}) fusion(f32[128,512,16]{1,2,0:T(8,128)S(1)} %fusion.49, f32[16,128]{0,1:T(8,128)S(1)} %copy.90, f32[16,128]{0,1:T(8,128)S(1)} %copy.87, f32[128,512,16]{1,2,0:T(8,128)S(1)} %fusion.27, f32[16,128,512]{2,1,0:T(8,128)S(1)} %bitcast.217), kind=kOutput, calls=%fused_computation.27 | convolution fusion | flops 208670208 | bytes 20987904 | tf_op jit(solution)/shard_map/kn,...nmq->...kmq/dot_general | solution.py:64
  291.1 6.3 fusion.19
  297.4 6.3 fusion.21
  303.7 6.8 fusion.55
  310.6 6.5 fusion.58
  317.1 4.2 maximum_bitcast_fusion.1
  321.3 11.4 %broadcast_multiply_fusion = f32[2,2,2048,512]{3,2,1,0:T(8,128)} fusion(f32[2,2048,512]{2,1,0:T(8,128)} %maximum_bitcast_fusion.1, f32[2]{0:T(128)S(1)} %fusion.191), kind=kLoop, calls=%fused_computation.16 | loop fusion | flops 4194304 | bytes 25165832 | tf_op jit(solution)/shard_map/lk,lcxq->kcxq/dot_general | solution.py:156
  332.7 17.1 %subtract_reduce_fusion = (f32[2048,512]{1,0:T(8,128)}, f32[2048,512]{1,0:T(8,128)}) fusion(f32[2,2,2048,512]{3,2,1,0:T(8,128)} %convert_element_type.136, f32[2,2,2048,512]{3,2,1,0:T(8,128)} %broadcast_multiply_fusion), kind=kLoop, calls=%fused_computation.15 | loop fusion | flops 14680064 | bytes 41943040 | tf_op jit(solution)/shard_map/reduce_sum | solution.py:158
  349.8 7.7 %pad_maximum_fusion = f32[2,2048,512]{2,1,0:T(8,128)} fusion(f32[1,2048,512]{2,1,0:T(8,128)} %bitcast.236, f32[1,2048,512]{2,1,0:T(8,128)} %bitcast.235), kind=kLoop, calls=%fused_computation.11 | loop fusion | flops 2097152 | bytes 16777216 | tf_op jit(solution)/shard_map/stack | solution.py:160
  357.5 0.0 all-reduce.2.cloned.1.call-update
  357.5 198.3 %all-reduce.2.cloned.1.call-done = f32[2,2048,512]{2,1,0:T(8,128)} async-done(((f32[2,2048,512]{2,1,0:T(8,128)}), f32[2,2048,512]{2,1,0:T(8,128)}) %all-reduce.2.cloned.1.call-update) | async-done | bytes 8388624 | tf_op jit(solution)/shard_map/psum | solution.py:166
  555.8 4.4 fusion.278
  560.2 4.3 fusion.92
  564.5 4.1 fusion.98
  568.6 4.6 convolution_subtract_fusion
  573.2 5.3 fusion.1
  578.5 6.2 fusion.11
  584.7 5.6 fusion.13
  590.3 5.8 fusion.61
  596.1 5.7 fusion.64
  601.8 2.4 copy.108
  604.3 2.4 copy.105
  606.7 0.7 copy_bitcast_fusion
  607.4 97.6 %all_to_all.15 = f32[4,256,2,512]{3,1,2,0:T(8,128)} all-to-all(f32[4,256,2,512]{3,1,2,0:T(8,128)S(1)} %copy_bitcast_fusion), channel_id=1, replica_groups=mesh['grp'=2,'pencil'=4,'depth'=2,'mem'=2] {'pencil'}, dimensions={0} | all-to-all | bytes 8388608 | tf_op jit(solution)/shard_map/all_to_all | solution.py:175
  705.0 5.3 copy.110
  710.3 2.5 fusion.280
  712.8 3.7 fusion.90
  716.5 3.6 fusion.88
  720.0 3.6 convolution_subtract_fusion.1
  723.7 4.0 multiply_subtract_fusion
  727.7 3.1 fusion.71
  730.8 3.2 multiply_bitcast_fusion
  733.9 1.5 mul.460
  (6 shorter events, 0.0 us)
Async XLA Ops:
  6.5 549.2 %all-reduce.2.cloned.1.call-start = ((), (), s32[]{:S(2)}) async-start(), calls=%async_computation.1 | async-start | bytes 16777216 | tf_op jit(solution)/shard_map/psum | solution.py:166
  57.6 52.0 %collective-permute-start.2 = (f32[1,2,512,512]{3,2,1,0:T(8,128)}, f32[1,2,512,512]{3,2,1,0:T(8,128)}, u32[]{:S(2)}, u32[]{:S(2)}) collective-permute-start(f32[1,2,512,512]{3,2,1,0:T(8,128)} %bitcast.243), channel_id=1, source_target_pairs={{0,12},{4,8},{8,4},{12,0},{1,13},{5,9},{9,5},{13,1},{2,14},{6,10},... | collective-permute-start | bytes 6291464 | tf_op jit(solution)/shard_map/ppermute | solution.py:144
  65.5 177.0 %collective-permute-start.1 = (f32[1,2,512,512]{3,2,1,0:T(8,128)}, f32[1,2,512,512]{3,2,1,0:T(8,128)}, u32[]{:S(2)}, u32[]{:S(2)}) collective-permute-start(f32[1,2,512,512]{3,2,1,0:T(8,128)} %bitcast.244), channel_id=1, source_target_pairs={{0,8},{4,12},{8,0},{12,4},{1,9},{5,13},{9,1},{13,5},{2,10},{6,14},... | collective-permute-start | bytes 6291464 | tf_op jit(solution)/shard_map/ppermute | solution.py:144
  68.5 174.1 %collective-permute-start = (f32[1,2,512,512]{3,2,1,0:T(8,128)}, f32[1,2,512,512]{3,2,1,0:T(8,128)}, u32[]{:S(2)}, u32[]{:S(2)}) collective-permute-start(f32[1,2,512,512]{3,2,1,0:T(8,128)} %bitcast.245), channel_id=1, source_target_pairs={{0,4},{4,0},{8,12},{12,8},{1,5},{5,1},{9,13},{13,9},{2,6},{6,2},{1... | collective-permute-start | bytes 6291464 | tf_op jit(solution)/shard_map/ppermute | solution.py:144
  71.7 170.9 %copy-start = (f32[1,2,512,1,512]{4,2,1,3,0:T(8,128)S(1)}, f32[1,2,512,1,512]{4,2,1,3,0:T(8,128)}, u32[]{:S(2)}) copy-start(f32[1,2,512,1,512]{4,2,1,3,0:T(8,128)} %copy.80) | copy-start | bytes 6291460
Sparse Core Ops, SparseCore 0:
  357.6 198.1 all-reduce.1
